TPU v7x, 512 devices: a whole 4x8x8 slice. The times are simulated.
512 devices in a mesh: slab: 64 (over x, z, core), filt: 8 (over y).
Axes of the slice: x: 4, y: 8, z: 8, core: 2. Of those that a mesh axis runs over, the one named last changes fastest.
Arguments:
- volume: bfloat16 [128, 128, 16, 256], P('slab', 'filt'), may hold values from -6 to 6
- weights: bfloat16 [3, 3, 3, 128, 256], replicated, may hold values from -0.109375 to 0.109375
- out_error: bfloat16 [64, 256, 8, 128], P('slab', 'filt'), may hold values from -6 to 6
Outputs:
- in_grad: bfloat16 [128, 128, 16, 256], P('slab', None, 'filt')
- weight_grad: float32 [3, 3, 3, 128, 256], P(None, None, None, None, 'filt')
All inputs are finite; a program needn't handle non-finite values.
Results may differ from a plain program's by a relative error of at most 0.0049.
Values may be sent and summed in bfloat16 or wider, within the bound.
No kernel may reach another device: no remote copies, remote signals or barrier semaphores. Data moves between devices by JAX's collectives and lax.ppermute only.
A program may use at most 64 MiB of HBM per device.

v0:
```python
import math
import jax
import jax.numpy as jnp
from jax import lax
from jax.sharding import PartitionSpec as P


def shifted_2(value, axis, steps):
    count = lax.axis_size(axis)
    first, last = (max(0, -steps), min(count, count - steps))
    return lax.ppermute(value, axis, [(source, source + steps) for source in range(first, last)])


def tap_pieces(extended, top):
    depth = (extended.shape[0] - 1) // 2
    rows = (extended.shape[2] + top - 1) // 2
    cols = extended.shape[3] // 2
    chans = extended.shape[1]
    padded = jnp.pad(extended, ((0, 1), (0, 0), (top, 1), (1, 1)))
    split = padded.reshape(depth + 1, 2, chans, rows + 1, 2, cols + 1, 2)
    pieces = []
    for a in range(3):
        for b in range(3):
            for c in range(3):
                piece = split[
                    a // 2 : a // 2 + depth,
                    a % 2,
                    :,
                    b // 2 : b // 2 + rows,
                    b % 2,
                    c // 2 : c // 2 + cols,
                    c % 2,
                ]
                pieces.append(((a, b, c), piece))
    return pieces


def forward_taps(pieces, kernel):
    total = None
    for (a, b, c), piece in pieces:
        term = jnp.einsum(
            "dkhw,kf->dfhw", piece, kernel[a, b, c], preferred_element_type=jnp.float32
        )
        total = term if total is None else total + term
    return total


def weight_taps(pieces, grad):
    terms = []
    for (a, b, c), piece in pieces:
        terms.append(jnp.einsum("dkhw,dfhw->kf", piece, grad, preferred_element_type=jnp.float32))
    stacked = jnp.stack(terms, 0)
    return stacked.reshape((3, 3, 3) + stacked.shape[1:])


def input_taps(grad_ext, kernel):
    depth = grad_ext.shape[0] - 1
    rows = grad_ext.shape[2] - 1
    cols = grad_ext.shape[3]
    chans = kernel.shape[3]
    parity_taps = ((1,), (2, 0))
    shifted = {}
    for a in range(3):
        for b in range(3):
            for c in range(3):
                term = jnp.einsum(
                    "dfhw,kf->dkhw", grad_ext, kernel[a, b, c], preferred_element_type=jnp.float32
                )
                start_d = 1 if a == 0 else 0
                start_r = 1 if b == 0 else 0
                term = term[start_d : start_d + depth, :, start_r : start_r + rows]
                if c == 0:
                    term = jnp.pad(term[..., 1:], ((0, 0), (0, 0), (0, 0), (0, 1)))
                shifted[a, b, c] = term
    depth_parts = []
    for even_d in range(2):
        row_parts = []
        for even_r in range(2):
            col_parts = []
            for even_c in range(2):
                total = None
                for a in parity_taps[even_d]:
                    for b in parity_taps[even_r]:
                        for c in parity_taps[even_c]:
                            total = shifted[a, b, c] if total is None else total + shifted[a, b, c]
                col_parts.append(total)
            row_parts.append(jnp.stack(col_parts, -1))
        row_parts = jnp.stack(row_parts, 3)
        depth_parts.append(row_parts)
    joined = jnp.stack(depth_parts, 1)
    return joined.reshape(2 * depth, chans, 2 * rows, 2 * cols)


def activation_grad(preact, error):
    sigma = jax.nn.sigmoid(preact)
    return (error * (sigma * (1.0 + preact * (1.0 - sigma)))).astype(jnp.bfloat16)


def on_device(volume, weights, out_error):
    member = lax.axis_index("filt")
    tile = out_error.shape[1]
    below = shifted_2(volume[-1:], "slab", 1)
    extended = jnp.concatenate([below, volume], 0)
    whole = lax.all_gather(extended, "filt", axis=1, tiled=True)
    pieces = tap_pieces(whole, 1)
    kernel_tile = lax.dynamic_slice_in_dim(weights, member * tile, tile, 4)
    preact = forward_taps(pieces, kernel_tile)
    grad = activation_grad(preact, out_error)
    weight_part = weight_taps(pieces, grad)
    grad_rows = lax.all_to_all(grad, "filt", split_axis=2, concat_axis=1, tiled=True)
    count = out_error.shape[0] * lax.axis_size("slab") * out_error.shape[2] * out_error.shape[3]
    weight_grad = lax.psum(weight_part, "slab") * (1.0 / math.sqrt(count))
    upper = shifted_2(grad_rows, "slab", -1)
    grad_ext = jnp.concatenate([grad_rows, upper], 0)
    right_row = shifted_2(grad_ext, "filt", -1)
    grad_ext = jnp.concatenate([grad_ext, right_row], 2)
    in_grad = input_taps(grad_ext, weights).astype(jnp.bfloat16)
    return (in_grad, weight_grad)


def solution(mesh):
    in_specs = (P("slab", "filt", None, None), P(), P("slab", "filt", None, None))
    out_specs = (P("slab", None, "filt", None), P(None, None, None, None, "filt"))
    return jax.shard_map(
        on_device, mesh=mesh, in_specs=in_specs, out_specs=out_specs, check_vma=False
    )
```

profile of v0, /device:TPU:1, one launch (start us, length us, event | category | flops | bytes accessed | tf_op | source)
XLA Modules:
  0.0 422.1 jit_solution(12113445541933201036)
XLA Ops:
  8.1 5.4 %collective-permute-start = (bf16[1,16,16,256]{3,2,1,0:T(8,128)(2,1)S(1)}, bf16[1,16,16,256]{3,2,1,0:T(8,128)(2,1)S(1)}, u32[]{:S(2)}, u32[]{:S(2)}) collective-permute-start(bf16[1,16,16,256]{3,2,1,0:T(8,128)(2,1)S(1)} %slice.347), channel_id=1, source_target_pairs={{0,8},{8,16},{16,24},{24,32},{32,40},{40,48},{48,56},{56,64},{64,7... | collective-permute-start | bytes 393224 | tf_op jit(solution)/shard_map/ppermute | solution.py:11
  13.5 3.6 collective-permute-done
  18.9 51.0 %all-gather.2.cloned.1.call-done = bf16[3,128,16,256]{3,2,1,0:T(8,128)(2,1)} async-done(((bf16[3,16,16,256]{3,2,1,0:T(8,128)(2,1)}), bf16[3,128,16,256]{3,2,1,0:T(8,128)(2,1)}) %all-gather.2.cloned.1.call-update) | async-done | bytes 3145744 | tf_op jit(solution)/shard_map/all_gather | solution.py:104
  69.9 6.1 %copy.203 = bf16[3,128,16,256]{1,0,3,2:T(4,128)(2,1)} copy(bf16[3,128,16,256]{3,2,1,0:T(8,128)(2,1)} %all-gather.2.cloned.1.call-done) | data formatting | bytes 6291456
  76.0 3.9 pad.32.clone
  79.9 4.1 fusion.214
  84.0 11.3 %fusion.213 = (bf16[1,1,128,8,1,128,1]{2,1,0,6,5,4,3:T(2,128)(2,1)}, bf16[1,1,128,8,1,128,1]{2,1,0,6,5,4,3:T(2,128)(2,1)}, bf16[1,1,128,8,1,128,1]{2,1,0,6,5,4,3...) fusion(bf16[2,2,128,9,2,129,2]{2,1,0,6,5,4,3:T(2,128)(2,1)S(1)}, ...), kind=kLoop, calls=%fused_computation.343 | loop fusion | bytes 9961472 | tf_op jit(solution)/shard_map/slice | solution.py:25
  97.4 1.9 copy.158
  101.2 1.9 copy.154
  103.0 1.9 copy.152
  104.9 1.9 copy.150
  106.8 1.9 copy.202
  118.8 1.9 copy.180
  120.7 1.9 copy.178
  122.6 1.9 copy.176
  124.5 1.9 copy.174
  126.3 1.9 copy.172
  128.2 1.9 copy.170
  130.1 1.9 copy.168
  132.0 1.9 copy.166
  165.6 4.6 %all-to-all-start = ((bf16[1,32,8,128]{3,1,0,2:T(8,128)(2,1)}), bf16[1,32,8,128]{3,1,0,2:T(8,128)(2,1)S(1)}, u32[]{:S(2)}, u32[]{:S(2)}) async-start(bf16[1,32,8,128]{3,1,0,2:T(8,128)(2,1)} %bitcast.83), calls=%async_computation | async-start | bytes 131072 | tf_op jit(solution)/shard_map/all_to_all | solution.py:110
  214.3 3.0 collective-permute-start.1
  217.3 3.2 collective-permute-done.1
  221.8 183.9 %all-reduce.12.cloned.1.call-done = f32[3,3,3,128,32]{3,4,2,1,0:T(8,128)} async-done(((f32[3,3,3,128,32]{3,4,2,1,0:T(8,128)}), f32[3,3,3,128,32]{3,4,2,1,0:T(8,128)}) %all-reduce.12.cloned.1.call-update) | async-done | bytes 442384 | tf_op jit(solution)/shard_map/psum | solution.py:112
  (175 shorter events, 102.6 us)
Async XLA Ops:
  7.2 62.7 %all-gather.2.cloned.1.call-start = ((), (), s32[]{:S(2)}) async-start(), calls=%async_computation.1 | async-start | bytes 3538944 | tf_op jit(solution)/shard_map/all_gather | solution.py:104
  8.1 9.0 %collective-permute-start = (bf16[1,16,16,256]{3,2,1,0:T(8,128)(2,1)S(1)}, bf16[1,16,16,256]{3,2,1,0:T(8,128)(2,1)S(1)}, u32[]{:S(2)}, u32[]{:S(2)}) collective-permute-start(bf16[1,16,16,256]{3,2,1,0:T(8,128)(2,1)S(1)} %slice.347), channel_id=1, source_target_pairs={{0,8},{8,16},{16,24},{24,32},{32,40},{40,48},{48,56},{56,64},{64,7... | collective-permute-start | bytes 393224 | tf_op jit(solution)/shard_map/ppermute | solution.py:11
  136.4 7.0 %copy-start.16 = (bf16[1,1,128,8,1,128,1]{5,2,3,6,4,1,0:T(8,128)(2,1)S(1)}, bf16[1,1,128,8,1,128,1]{5,2,3,6,4,1,0:T(8,128)(2,1)}, u32[]{:S(2)}) copy-start(bf16[1,1,128,8,1,128,1]{5,2,3,6,4,1,0:T(8,128)(2,1)} %copy.166) | copy-start | bytes 786436
  137.7 6.8 %copy-start.14 = (bf16[1,1,128,8,1,128,1]{5,2,3,6,4,1,0:T(8,128)(2,1)S(1)}, bf16[1,1,128,8,1,128,1]{5,2,3,6,4,1,0:T(8,128)(2,1)}, u32[]{:S(2)}) copy-start(bf16[1,1,128,8,1,128,1]{5,2,3,6,4,1,0:T(8,128)(2,1)} %copy.168) | copy-start | bytes 786436
  139.0 6.5 %copy-start.11 = (bf16[1,1,128,8,1,128,1]{5,2,3,6,4,1,0:T(8,128)(2,1)S(1)}, bf16[1,1,128,8,1,128,1]{5,2,3,6,4,1,0:T(8,128)(2,1)}, u32[]{:S(2)}) copy-start(bf16[1,1,128,8,1,128,1]{5,2,3,6,4,1,0:T(8,128)(2,1)} %copy.170) | copy-start | bytes 786436
  140.1 6.5 %copy-start.9 = (bf16[1,1,128,8,1,128,1]{5,2,3,6,4,1,0:T(8,128)(2,1)S(1)}, bf16[1,1,128,8,1,128,1]{5,2,3,6,4,1,0:T(8,128)(2,1)}, u32[]{:S(2)}) copy-start(bf16[1,1,128,8,1,128,1]{5,2,3,6,4,1,0:T(8,128)(2,1)} %copy.172) | copy-start | bytes 786436
  141.1 6.5 %copy-start.7 = (bf16[1,1,128,8,1,128,1]{5,2,3,6,4,1,0:T(8,128)(2,1)S(1)}, bf16[1,1,128,8,1,128,1]{5,2,3,6,4,1,0:T(8,128)(2,1)}, u32[]{:S(2)}) copy-start(bf16[1,1,128,8,1,128,1]{5,2,3,6,4,1,0:T(8,128)(2,1)} %copy.174) | copy-start | bytes 786436
  142.2 6.4 %copy-start.5 = (bf16[1,1,128,8,1,128,1]{5,2,3,6,4,1,0:T(8,128)(2,1)S(1)}, bf16[1,1,128,8,1,128,1]{5,2,3,6,4,1,0:T(8,128)(2,1)}, u32[]{:S(2)}) copy-start(bf16[1,1,128,8,1,128,1]{5,2,3,6,4,1,0:T(8,128)(2,1)} %copy.176) | copy-start | bytes 786436
  143.3 6.4 %copy-start.3 = (bf16[1,1,128,8,1,128,1]{5,2,3,6,4,1,0:T(8,128)(2,1)S(1)}, bf16[1,1,128,8,1,128,1]{5,2,3,6,4,1,0:T(8,128)(2,1)}, u32[]{:S(2)}) copy-start(bf16[1,1,128,8,1,128,1]{5,2,3,6,4,1,0:T(8,128)(2,1)} %copy.178) | copy-start | bytes 786436
  157.0 7.0 %copy-start.13 = (bf16[1,1,128,8,1,128,1]{5,2,3,6,4,1,0:T(8,128)(2,1)S(1)}, bf16[1,1,128,8,1,128,1]{5,2,3,6,4,1,0:T(8,128)(2,1)}, u32[]{:S(2)}) copy-start(bf16[1,1,128,8,1,128,1]{5,2,3,6,4,1,0:T(8,128)(2,1)} %copy.150) | copy-start | bytes 786436
  165.6 48.6 %all-to-all-start = ((bf16[1,32,8,128]{3,1,0,2:T(8,128)(2,1)}), bf16[1,32,8,128]{3,1,0,2:T(8,128)(2,1)S(1)}, u32[]{:S(2)}, u32[]{:S(2)}) async-start(bf16[1,32,8,128]{3,1,0,2:T(8,128)(2,1)} %bitcast.83), calls=%async_computation | async-start | bytes 131072 | tf_op jit(solution)/shard_map/all_to_all | solution.py:110
  170.3 235.4 %all-reduce.12.cloned.1.call-start = ((), (), s32[]{:S(2)}) async-start(), calls=%async_computation.2 | async-start | bytes 884736 | tf_op jit(solution)/shard_map/psum | solution.py:112
  170.5 12.3 %copy-start.17 = (bf16[1,1,128,8,1,128,1]{5,2,3,6,4,1,0:T(8,128)(2,1)S(1)}, bf16[1,1,128,8,1,128,1]{5,2,3,6,4,1,0:T(8,128)(2,1)}, u32[]{:S(2)}) copy-start(bf16[1,1,128,8,1,128,1]{5,2,3,6,4,1,0:T(8,128)(2,1)} %copy.166) | copy-start | bytes 786436
  170.5 13.9 %copy-start.15 = (bf16[1,1,128,8,1,128,1]{5,2,3,6,4,1,0:T(8,128)(2,1)S(1)}, bf16[1,1,128,8,1,128,1]{5,2,3,6,4,1,0:T(8,128)(2,1)}, u32[]{:S(2)}) copy-start(bf16[1,1,128,8,1,128,1]{5,2,3,6,4,1,0:T(8,128)(2,1)} %copy.168) | copy-start | bytes 786436
  170.5 15.5 %copy-start.12 = (bf16[1,1,128,8,1,128,1]{5,2,3,6,4,1,0:T(8,128)(2,1)S(1)}, bf16[1,1,128,8,1,128,1]{5,2,3,6,4,1,0:T(8,128)(2,1)}, u32[]{:S(2)}) copy-start(bf16[1,1,128,8,1,128,1]{5,2,3,6,4,1,0:T(8,128)(2,1)} %copy.170) | copy-start | bytes 786436
  170.5 17.2 %copy-start.10 = (bf16[1,1,128,8,1,128,1]{5,2,3,6,4,1,0:T(8,128)(2,1)S(1)}, bf16[1,1,128,8,1,128,1]{5,2,3,6,4,1,0:T(8,128)(2,1)}, u32[]{:S(2)}) copy-start(bf16[1,1,128,8,1,128,1]{5,2,3,6,4,1,0:T(8,128)(2,1)} %copy.172) | copy-start | bytes 786436
  172.4 17.0 %copy-start.8 = (bf16[1,1,128,8,1,128,1]{5,2,3,6,4,1,0:T(8,128)(2,1)S(1)}, bf16[1,1,128,8,1,128,1]{5,2,3,6,4,1,0:T(8,128)(2,1)}, u32[]{:S(2)}) copy-start(bf16[1,1,128,8,1,128,1]{5,2,3,6,4,1,0:T(8,128)(2,1)} %copy.174) | copy-start | bytes 786436
  174.2 16.8 %copy-start.6 = (bf16[1,1,128,8,1,128,1]{5,2,3,6,4,1,0:T(8,128)(2,1)S(1)}, bf16[1,1,128,8,1,128,1]{5,2,3,6,4,1,0:T(8,128)(2,1)}, u32[]{:S(2)}) copy-start(bf16[1,1,128,8,1,128,1]{5,2,3,6,4,1,0:T(8,128)(2,1)} %copy.176) | copy-start | bytes 786436
  176.0 16.7 %copy-start.4 = (bf16[1,1,128,8,1,128,1]{5,2,3,6,4,1,0:T(8,128)(2,1)S(1)}, bf16[1,1,128,8,1,128,1]{5,2,3,6,4,1,0:T(8,128)(2,1)}, u32[]{:S(2)}) copy-start(bf16[1,1,128,8,1,128,1]{5,2,3,6,4,1,0:T(8,128)(2,1)} %copy.178) | copy-start | bytes 786436
  177.8 16.5 %copy-start.2 = (bf16[1,1,128,8,1,128,1]{5,2,3,6,4,1,0:T(8,128)(2,1)S(1)}, bf16[1,1,128,8,1,128,1]{5,2,3,6,4,1,0:T(8,128)(2,1)}, u32[]{:S(2)}) copy-start(bf16[1,1,128,8,1,128,1]{5,2,3,6,4,1,0:T(8,128)(2,1)} %copy.180) | copy-start | bytes 786436
  195.9 16.6 %copy-start.19 = (bf16[1,1,128,8,1,128,1]{5,2,3,6,4,1,0:T(8,128)(2,1)S(1)}, bf16[1,1,128,8,1,128,1]{5,2,3,6,4,1,0:T(8,128)(2,1)}, u32[]{:S(2)}) copy-start(bf16[1,1,128,8,1,128,1]{5,2,3,6,4,1,0:T(8,128)(2,1)} %copy.202) | copy-start | bytes 786436
  207.5 200.0 %copy-start.20 = (bf16[3,3,3,128,256]{4,3,2,1,0:T(8,128)(2,1)S(1)}, bf16[3,3,3,128,256]{4,3,2,1,0:T(8,128)(2,1)}, u32[]{:S(2)}) copy-start(bf16[3,3,3,128,256]{4,3,2,1,0:T(8,128)(2,1)} %param.4) | copy-start | bytes 5308420
  214.3 6.1 %collective-permute-start.1 = (bf16[1,256,1,128]{1,3,2,0:T(8,128)(2,1)S(1)}, bf16[1,256,1,128]{1,3,2,0:T(8,128)(2,1)S(1)}, u32[]{:S(2)}, u32[]{:S(2)}) collective-permute-start(bf16[1,256,1,128]{1,3,2,0:T(8,128)(2,1)S(1)} %copy.115), channel_id=1, source_target_pairs={{8,0},{16,8},{24,16},{32,24},{40,32},{48,40},{56,48},{64,56},{72,6... | collective-permute-start | bytes 196616 | tf_op jit(solution)/shard_map/ppermute | solution.py:11
  220.5 187.0 %collective-permute-start.2 = (bf16[2,256,1,128]{1,3,2,0:T(8,128)(2,1)S(1)}, bf16[2,256,1,128]{1,3,2,0:T(8,128)(2,1)S(1)}, u32[]{:S(2)}, u32[]{:S(2)}) collective-permute-start(bf16[2,256,1,128]{1,3,2,0:T(8,128)(2,1)S(1)} %pad_maximum_fusion.2), channel_id=1, source_target_pairs={{1,0},{2,1},{3,2},{4,3},{5,4},{6,5},{7,6},{9,8},{10,9},{11,10},{12... | collective-permute-start | bytes 393224 | tf_op jit(solution)/shard_map/ppermute | solution.py:11
  (4 other events, 24.1 us)
Sparse Core Ops, SparseCore 0:
  19.0 50.8 all-gather.1
  214.3 191.2 all-reduce.11
where the time goes:
time: 425 us; the launch traced here: 422 us
  waiting for transfers between devices  242 us (57%)
  matrix products  80.7 us (19%)
  local copies, waits for them, and re-layouts  66.4 us (16%)
  between operations  15 us (4%)
  starting transfers between devices  14.5 us (3%)
    psum x1, waiting for transfers between devices, on_device(): weight_grad = lax.psum(weight_part, 'slab') * (1.0 / math.sqrt(count))  184 us
    all_gather x1, waiting for transfers between devices, on_device(): whole = lax.all_gather(extended, 'filt', axis=1, tiled=True)  51 us
    unnamed x73, local copies, waits for them, and re-layouts  45.6 us
    dot_general x27, matrix products, weight_taps(): jnp.einsum('dkhw,dfhw->kf', piece, grad, preferred_element_type=jnp.float32)  45.2 us
    dot_general x27, matrix products, forward_taps(): jnp.einsum('dkhw,kf->dfhw', piece, kernel[a, b, c], preferred_element_typ...  29.6 us
    slice x2, local copies, waits for them, and re-layouts, tap_pieces(): split[a // 2:a // 2 + depth, a % 2, :, b // 2:b // 2 + rows, b % 2, c //...  15.4 us
    ppermute x3, starting transfers between devices, shifted_2(): lax.ppermute(value, axis, [(source, source + steps) for source in range(f...  9.64 us
  transfers between devices with their start and end apart: 6, of which 4 were waited for; matrix products, arithmetic and copies ran while one was open for 11% of the time, Pallas kernels for 0%

commit v1 on v0

--- a/solution.py
+++ b/solution.py
@@ -101,7 +101,23 @@
     tile = out_error.shape[1]
     below = shifted_2(volume[-1:], "slab", 1)
     extended = jnp.concatenate([below, volume], 0)
-    whole = lax.all_gather(extended, "filt", axis=1, tiled=True)
+    ways, here, lap = (lax.axis_size("filt"), lax.axis_index("filt"), extended.shape[1])
+    shape = [n * ways if d == 1 else n for d, n in enumerate(extended.shape)]
+    full = lax.dynamic_update_slice_in_dim(
+        jnp.zeros(shape, extended.dtype), extended, here * lap, axis=1
+    )
+    going_up = going_down = extended
+    for far in range(1, ways // 2 + 1):
+        going_up = lax.ppermute(going_up, "filt", [(d, (d + 1) % ways) for d in range(ways)])
+        full = lax.dynamic_update_slice_in_dim(full, going_up, (here - far) % ways * lap, axis=1)
+        if 2 * far < ways:
+            going_down = lax.ppermute(
+                going_down, "filt", [(d, (d - 1) % ways) for d in range(ways)]
+            )
+            full = lax.dynamic_update_slice_in_dim(
+                full, going_down, (here + far) % ways * lap, axis=1
+            )
+    whole = full
     pieces = tap_pieces(whole, 1)
     kernel_tile = lax.dynamic_slice_in_dim(weights, member * tile, tile, 4)
     preact = forward_taps(pieces, kernel_tile)

time: 425 us -> 5290 us (12.45)
  local copies, waits for them, and re-layouts: 66.4 us -> 4940 us
    dynamic_update_slice x0 -> x8, local copies, waits for them, and re-layouts: none -> 4850 us  [the longest x4 2700 us: on_device(): lax.dynamic_update_slice_in_dim(full, going_up, (here - far) % ways * lap...]
  transfers between devices with their start and end apart: 6 -> 12, of which waited for: 4 -> 6; matrix products, arithmetic and copies ran while one was open for 11% -> 80% of each run, Pallas kernels for 0% -> 0%
where the time goes in v1:
time: 5290 us
  local copies, waits for them, and re-layouts  4940 us (93%)
  waiting for transfers between devices  214 us (4%)
  matrix products  80.8 us (2%)
    dynamic_update_slice x4, local copies, waits for them, and re-layouts, on_device(): lax.dynamic_update_slice_in_dim(full, going_up, (here - far) % ways * lap...  2700 us
    dynamic_update_slice x3, local copies, waits for them, and re-layouts, on_device(): lax.dynamic_update_slice_in_dim(full, going_down, (here + far) % ways * l...  2020 us
    psum x1, waiting for transfers between devices, on_device(): weight_grad = lax.psum(weight_part, 'slab') * (1.0 / math.sqrt(count))  186 us
    dynamic_update_slice x1, local copies, waits for them, and re-layouts, on_device(): lax.dynamic_update_slice_in_dim(jnp.zeros(shape, extended.dtype), extende...  123 us
  transfers between devices with their start and end apart: 12, of which 6 were waited for; matrix products, arithmetic and copies ran while one was open for 80% of the time, Pallas kernels for 0%

profile of v1, /device:TPU:1, one launch (start us, length us, event | category | flops | bytes accessed | tf_op | source)
XLA Modules:
  0.0 5288.3 jit_solution(9816795602712230355)
XLA Ops:
  8.1 5.4 collective-permute-start
  13.5 3.6 collective-permute-done
  20.0 4.6 collective-permute-start.2
  24.6 7.2 collective-permute-done.1
  33.7 4.6 collective-permute-start.4
  38.2 6.2 collective-permute-done.3
  46.4 4.6 collective-permute-start.6
  51.0 5.3 collective-permute-done.5
  61.9 3.6 broadcast_in_dim.3
  65.5 123.1 %dynamic_update_slice.24 = bf16[3,128,16,256]{1,0,3,2:T(4,128)(2,1)} dynamic-update-slice(bf16[3,128,16,256]{1,0,3,2:T(4,128)(2,1)} %broadcast_in_dim.3, bf16[3,16,16,256]{1,0,3,2:T(4,128)(2,1)} %copy.99, s32[]{:T(128)} %constant.56.clone.1, s32[]{:T(128)S(6)} %select_n.59, s32[]{:T(128)} %constant.56.clone.1, s32[]{:T(128)} %constant.56.clone.1) | dynamic-update-slice | bytes 786436 | tf_op jit(solution)/shard_map/dynamic_update_slice | solution.py:106
  192.2 674.7 %dynamic_update_slice.25 = bf16[3,128,16,256]{1,0,3,2:T(4,128)(2,1)} dynamic-update-slice(bf16[3,128,16,256]{1,0,3,2:T(4,128)(2,1)} %dynamic_update_slice.24, bf16[3,16,16,256]{1,0,3,2:T(4,128)(2,1)} %copy.100, s32[]{:T(128)} %constant.56.clone.1, s32[]{:T(128)S(6)} %select_n.61, s32[]{:T(128)} %constant.56.clone.1, s32[]{:T(128)} %constant.56.clone.1) | dynamic-update-slice | bytes 786436 | tf_op jit(solution)/shard_map/dynamic_update_slice | solution.py:112
  870.4 674.7 %dynamic_update_slice.26 = bf16[3,128,16,256]{1,0,3,2:T(4,128)(2,1)} dynamic-update-slice(bf16[3,128,16,256]{1,0,3,2:T(4,128)(2,1)} %dynamic_update_slice.25, bf16[3,16,16,256]{1,0,3,2:T(4,128)(2,1)} %copy.101, s32[]{:T(128)} %constant.56.clone.1, s32[]{:T(128)S(6)} %select_n.63, s32[]{:T(128)} %constant.56.clone.1, s32[]{:T(128)} %constant.56.clone.1) | dynamic-update-slice | bytes 786436 | tf_op jit(solution)/shard_map/dynamic_update_slice | solution.py:117
  1548.7 674.7 %dynamic_update_slice.27 = bf16[3,128,16,256]{1,0,3,2:T(4,128)(2,1)} dynamic-update-slice(bf16[3,128,16,256]{1,0,3,2:T(4,128)(2,1)} %dynamic_update_slice.26, bf16[3,16,16,256]{1,0,3,2:T(4,128)(2,1)} %copy.102, s32[]{:T(128)} %constant.56.clone.1, s32[]{:T(128)S(6)} %select_n.65, s32[]{:T(128)} %constant.56.clone.1, s32[]{:T(128)} %constant.56.clone.1) | dynamic-update-slice | bytes 786436 | tf_op jit(solution)/shard_map/dynamic_update_slice | solution.py:112
  2227.0 674.7 %dynamic_update_slice.28 = bf16[3,128,16,256]{1,0,3,2:T(4,128)(2,1)} dynamic-update-slice(bf16[3,128,16,256]{1,0,3,2:T(4,128)(2,1)} %dynamic_update_slice.27, bf16[3,16,16,256]{1,0,3,2:T(4,128)(2,1)} %copy.103, s32[]{:T(128)} %constant.56.clone.1, s32[]{:T(128)S(6)} %select_n.67, s32[]{:T(128)} %constant.56.clone.1, s32[]{:T(128)} %constant.56.clone.1) | dynamic-update-slice | bytes 786436 | tf_op jit(solution)/shard_map/dynamic_update_slice | solution.py:117
  2905.3 674.7 %dynamic_update_slice.29 = bf16[3,128,16,256]{1,0,3,2:T(4,128)(2,1)} dynamic-update-slice(bf16[3,128,16,256]{1,0,3,2:T(4,128)(2,1)} %dynamic_update_slice.28, bf16[3,16,16,256]{1,0,3,2:T(4,128)(2,1)} %copy.104, s32[]{:T(128)} %constant.56.clone.1, s32[]{:T(128)S(6)} %select_n.69, s32[]{:T(128)} %constant.56.clone.1, s32[]{:T(128)} %constant.56.clone.1) | dynamic-update-slice | bytes 786436 | tf_op jit(solution)/shard_map/dynamic_update_slice | solution.py:112
  3583.6 674.7 %dynamic_update_slice.30 = bf16[3,128,16,256]{1,0,3,2:T(4,128)(2,1)} dynamic-update-slice(bf16[3,128,16,256]{1,0,3,2:T(4,128)(2,1)} %dynamic_update_slice.29, bf16[3,16,16,256]{1,0,3,2:T(4,128)(2,1)} %copy.105, s32[]{:T(128)} %constant.56.clone.1, s32[]{:T(128)S(6)} %select_n.71, s32[]{:T(128)} %constant.56.clone.1, s32[]{:T(128)} %constant.56.clone.1) | dynamic-update-slice | bytes 786436 | tf_op jit(solution)/shard_map/dynamic_update_slice | solution.py:117
  4261.8 674.9 %dynamic_update_slice.31 = bf16[3,128,16,256]{1,0,3,2:T(4,128)(2,1)} dynamic-update-slice(bf16[3,128,16,256]{1,0,3,2:T(4,128)(2,1)} %dynamic_update_slice.30, bf16[3,16,16,256]{1,0,3,2:T(4,128)(2,1)} %copy.106, s32[]{:T(128)} %constant.56.clone.1, s32[]{:T(128)S(6)} %select_n.73, s32[]{:T(128)} %constant.56.clone.1, s32[]{:T(128)} %constant.56.clone.1) | dynamic-update-slice | bytes 786436 | tf_op jit(solution)/shard_map/dynamic_update_slice | solution.py:112
  4936.8 4.0 pad.32
  4940.7 4.9 fusion.214
  4945.7 11.0 fusion.213
  5025.9 4.3 all-to-all-start
  5074.2 4.9 collective-permute-start.8
  5079.1 4.7 collective-permute-done.8
  5085.4 186.5 %all-reduce.12.cloned.1.call-done = f32[3,3,3,128,32]{3,4,2,1,0:T(8,128)} async-done(((f32[3,3,3,128,32]{3,4,2,1,0:T(8,128)}), f32[3,3,3,128,32]{3,4,2,1,0:T(8,128)}) %all-reduce.12.cloned.1.call-update) | async-done | bytes 442384 | tf_op jit(solution)/shard_map/psum | solution.py:128
  (199 shorter events, 161.2 us)
Async XLA Ops:
  8.1 9.0 collective-permute-start
  18.1 13.7 collective-permute-start.1
  20.0 13.7 collective-permute-start.2
  31.7 12.7 collective-permute-start.3
  33.7 12.7 collective-permute-start.4
  44.5 11.8 collective-permute-start.5
  46.4 3533.6 %collective-permute-start.6 = (bf16[3,16,16,256]{3,2,1,0:T(8,128)(2,1)S(1)}, bf16[3,16,16,256]{3,2,1,0:T(8,128)(2,1)S(1)}, u32[]{:S(2)}, u32[]{:S(2)}) collective-permute-start(bf16[3,16,16,256]{3,2,1,0:T(8,128)(2,1)S(1)} %collective-permute-done.4), channel_id=1, source_target_pairs={{0,7},{1,0},{2,1},{3,2},{4,3},{5,4},{6,5},{7,6},{8,15},{9,8},{10,9... | collective-permute-start | bytes 1179656 | tf_op jit(solution)/shard_map/ppermute | solution.py:114
  56.3 4202.0 %collective-permute-start.7 = (bf16[3,16,16,256]{3,2,1,0:T(8,128)(2,1)S(1)}, bf16[3,16,16,256]{3,2,1,0:T(8,128)(2,1)S(1)}, u32[]{:S(2)}, u32[]{:S(2)}) collective-permute-start(bf16[3,16,16,256]{3,2,1,0:T(8,128)(2,1)S(1)} %collective-permute-done.5), channel_id=1, source_target_pairs={{0,1},{1,2},{2,3},{3,4},{4,5},{5,6},{6,7},{7,0},{8,9},{9,10},{10,1... | collective-permute-start | bytes 1179656 | tf_op jit(solution)/shard_map/ppermute | solution.py:111
  4994.2 7.4 copy-start.10
  4995.5 7.2 copy-start.11
  4996.8 7.0 copy-start.8
  5017.3 7.0 copy-start.15
  5025.9 48.2 all-to-all-start
  5030.2 241.6 %all-reduce.12.cloned.1.call-start = ((), (), s32[]{:S(2)}) async-start(), calls=%async_computation.1 | async-start | bytes 884736 | tf_op jit(solution)/shard_map/psum | solution.py:128
  5030.3 10.7 copy-start.12
  5030.3 12.4 copy-start.9
  5030.3 14.0 copy-start.7
  5030.3 15.6 copy-start.5
  5030.3 17.3 copy-start.3
  5032.2 17.1 copy-start.1
  5055.8 16.6 copy-start.17
  5065.7 207.9 %copy-start.18 = (bf16[3,3,3,128,256]{4,3,2,1,0:T(8,128)(2,1)S(1)}, bf16[3,3,3,128,256]{4,3,2,1,0:T(8,128)(2,1)}, u32[]{:S(2)}) copy-start(bf16[3,3,3,128,256]{4,3,2,1,0:T(8,128)(2,1)} %param.4) | copy-start | bytes 5308420
  5074.2 9.6 collective-permute-start.8
  5083.8 189.8 %collective-permute-start.9 = (bf16[2,256,1,128]{1,3,2,0:T(8,128)(2,1)S(1)}, bf16[2,256,1,128]{1,3,2,0:T(8,128)(2,1)S(1)}, u32[]{:S(2)}, u32[]{:S(2)}) collective-permute-start(bf16[2,256,1,128]{1,3,2,0:T(8,128)(2,1)S(1)} %pad_maximum_fusion.1), channel_id=1, source_target_pairs={{1,0},{2,1},{3,2},{4,3},{5,4},{6,5},{7,6},{9,8},{10,9},{11,10},{12... | collective-permute-start | bytes 393224 | tf_op jit(solution)/shard_map/ppermute | solution.py:11
  (8 other events, 50.0 us)
Sparse Core Ops, SparseCore 0:
  5074.2 197.5 all-reduce.11
